TPU v7x, 32 devices: a whole 2x2x4 slice. The times are simulated.
32 devices in a mesh: grp: 4 (over y, x), row: 8 (over z, core).
Axes of the slice: x: 2, y: 2, z: 4, core: 2. Of those that a mesh axis runs over, the one named last changes fastest.
Arguments:
- snapshots: float32 [16, 4, 65536], P('grp', None, 'row'), may hold values from -12 to 12
- basis: float32 [128, 262144], P(None, ('grp', 'row')), may hold values from -4 to 4
- assignment: int32 [16], replicated, may hold values from 0 to 15, each once
- param_index: int32 [16], replicated, may hold values from 0 to 63
- offsets: int32 [8, 262144], P(None, ('grp', 'row')), may hold values from -2048 to 2048, as said below
- coefs: float32 [2, 8, 262144], P(None, None, ('grp', 'row')), may hold values from -2.5 to 2.5
Outputs:
- new_columns: float32 [16, 262144], P(None, ('grp', 'row'))
- applied: float32 [2, 16, 262144], P(None, None, ('grp', 'row'))
- coords: float32 [128, 16], replicated
- r_factor: float32 [16, 16], replicated
- reduced: float32 [2, 144, 16], replicated
- estimate: float32 [16], replicated
Inputs may be any that keep to these rules, and one draw needn't show every extreme that they name: `offsets`: both ends of the range occur in every draw.
All inputs are finite; a program needn't handle non-finite values.
Results may differ from a plain program's by a relative error of at most 0.00029.
Values sent between devices are 32-bit elements; how exact they have to be, the bound alone decides.
A program may use at most 64 MiB of HBM per device.

v0:
```python
import jax
import jax.numpy as jnp
from jax import lax
from jax.sharding import PartitionSpec as P

NPARAM = 64


def extended_2(block, sides, width):
    for axis, dim in sides:
        count = lax.axis_size(axis)
        forward = [(i, i + 1) for i in range(count - 1)]
        backward = [(target, source) for source, target in forward]
        low = lax.ppermute(
            lax.slice_in_dim(block, block.shape[dim] - width, None, axis=dim), axis, forward
        )
        high = lax.ppermute(lax.slice_in_dim(block, 0, width, axis=dim), axis, backward)
        block = jnp.concatenate([low, block, high], axis=dim)
    return block


def cholesky_lower(matrix):
    order = matrix.shape[0]
    index_list = jnp.arange(order, dtype=jnp.int32)

    def cholesky_step(column_index, factor):
        column = lax.dynamic_slice_in_dim(matrix, column_index, 1, 1)[:, 0]
        factor_row = lax.dynamic_slice_in_dim(factor, column_index, 1, 0)[0]
        column = column - jnp.dot(factor, factor_row, precision=lax.Precision.HIGHEST)
        pivot = jnp.sqrt(jnp.sum(jnp.where(index_list == column_index, column, 0.0)))
        fresh = jnp.where(
            index_list > column_index,
            column / pivot,
            jnp.where(index_list == column_index, pivot, 0.0),
        )
        return lax.dynamic_update_slice_in_dim(factor, fresh[:, None], column_index, 1)

    return lax.fori_loop(0, order, cholesky_step, jnp.zeros(matrix.shape, matrix.dtype))


def forward_solve(lower, right):
    order = lower.shape[0]

    def forward_step(row_index, solved):
        lower_row = lax.dynamic_slice_in_dim(lower, row_index, 1, 0)[0]
        pivot = jnp.sum(jnp.where(jnp.arange(order, dtype=jnp.int32) == row_index, lower_row, 0.0))
        target = lax.dynamic_slice_in_dim(right, row_index, 1, 0)[0]
        value = (target - jnp.dot(lower_row, solved, precision=lax.Precision.HIGHEST)) / pivot
        return lax.dynamic_update_slice_in_dim(solved, value[None, :], row_index, 0)

    return lax.fori_loop(0, order, forward_step, jnp.zeros(right.shape, right.dtype))


def backward_solve(lower, right):
    order = lower.shape[0]

    def backward_step(turn, solved):
        row_index = order - 1 - turn
        upper_row = lax.dynamic_slice_in_dim(lower, row_index, 1, 1)[:, 0]
        pivot = jnp.sum(jnp.where(jnp.arange(order, dtype=jnp.int32) == row_index, upper_row, 0.0))
        target = lax.dynamic_slice_in_dim(right, row_index, 1, 0)[0]
        value = (target - jnp.dot(upper_row, solved, precision=lax.Precision.HIGHEST)) / pivot
        return lax.dynamic_update_slice_in_dim(solved, value[None, :], row_index, 0)

    return lax.fori_loop(0, order, backward_step, jnp.zeros(right.shape, right.dtype))


def apply_local(extended, offsets, coefs, width):
    row_count = offsets.shape[1]
    positions = jnp.arange(row_count, dtype=jnp.int32) + width
    totals = [
        jnp.zeros((extended.shape[0], row_count), jnp.float32)
        for term_index in range(coefs.shape[0])
    ]
    for slot_index in range(offsets.shape[0]):
        picked = jnp.take(extended, positions + offsets[slot_index], axis=1)
        totals = [
            totals[term_index] + coefs[term_index, slot_index][None, :] * picked
            for term_index in range(len(totals))
        ]
    return jnp.stack(totals)


def body(snapshots, basis, assignment, param_index, offsets, coefs):
    highest = lax.Precision.HIGHEST
    snap_count = assignment.shape[0]
    local_rows = basis.shape[1]
    total_rows = local_rows * lax.axis_size("grp") * lax.axis_size("row")
    width = local_rows // 4
    received = lax.all_to_all(snapshots, "grp", split_axis=1, concat_axis=0, tiled=True)
    arrived = received.reshape(snap_count, local_rows)
    placing = (assignment[None, :] == jnp.arange(snap_count, dtype=jnp.int32)[:, None]).astype(
        jnp.float32
    )
    ordered = jnp.dot(placing, arrived, precision=highest)
    gram = lax.psum(jnp.dot(basis, basis.T, precision=highest), ("grp", "row")) / total_rows
    basis_lower = cholesky_lower(gram)
    project_sum, snap_sum = lax.psum(
        (
            jnp.dot(basis, ordered.T, precision=highest),
            jnp.dot(ordered, ordered.T, precision=highest),
        ),
        ("grp", "row"),
    )
    project = project_sum / total_rows
    halfway = forward_solve(basis_lower, project)
    coords = backward_solve(basis_lower, halfway)
    residual = ordered - jnp.dot(coords.T, basis, precision=highest)
    cross = jnp.dot(project.T, coords, precision=highest)
    curved = jnp.dot(coords.T, jnp.dot(gram, coords, precision=highest), precision=highest)
    residual_gram = snap_sum / total_rows - cross - cross.T + curved
    residual_gram = 0.5 * (residual_gram + residual_gram.T)
    lower = cholesky_lower(residual_gram)
    inverse = forward_solve(lower, jnp.eye(snap_count, dtype=jnp.float32))
    new_columns = jnp.dot(inverse, residual, precision=highest)
    extended = extended_2(new_columns, ((("grp", "row"), 1),), width)
    applied = apply_local(extended, offsets, coefs, width)
    blocks = []
    for term_index in range(coefs.shape[0]):
        upper_part = jnp.dot(basis, applied[term_index].T, precision=highest)
        lower_part = jnp.dot(new_columns, applied[term_index].T, precision=highest)
        blocks.append(jnp.concatenate([upper_part, lower_part], axis=0))
    viscosity = 0.5 + param_index.astype(jnp.float32) / NPARAM
    combined = applied[0]
    term_index = 1
    combined = combined + (viscosity**term_index)[:, None] * applied[term_index]
    block_sum, square_sum = lax.psum(
        (jnp.stack(blocks), jnp.sum(combined * combined, axis=1)), ("grp", "row")
    )
    reduced = block_sum / total_rows
    estimate = square_sum / total_rows
    return (new_columns, applied, coords, lower.T, reduced, estimate)


def solution(mesh):
    return jax.shard_map(
        body,
        mesh=mesh,
        in_specs=(
            P("grp", None, "row"),
            P(None, ("grp", "row")),
            P(),
            P(),
            P(None, ("grp", "row")),
            P(None, None, ("grp", "row")),
        ),
        out_specs=(P(None, ("grp", "row")), P(None, None, ("grp", "row")), P(), P(), P(), P()),
        check_vma=False,
    )
```

profile of v0, /device:TPU:0, one launch (start us, length us, event | category | flops | bytes accessed | tf_op | source)
XLA Modules:
  0.0 1223.7 jit_solution(2992273450105122434)
XLA Ops:
  7.2 2.2 copy.74
  9.3 5.2 all-to-all-start
  14.6 7.6 fusion.64
  24.5 1.1 fusion.60
  25.6 116.0 %all-reduce.4.cloned.1.call-done = f32[128,128]{1,0:T(8,128)} async-done(((f32[128,128]{1,0:T(8,128)}), f32[128,128]{1,0:T(8,128)}) %all-reduce.4.cloned.1.call-update) | async-done | bytes 65552 | tf_op jit(solution)/shard_map/psum | solution.py:96
  141.6 0.8 broadcast_multiply_fusion
  142.6 258.7 %while.74 = (s32[]{:T(128)}, f32[128,128]{1,0:T(8,128)S(1)}, f32[128,128]{0,1:T(8,128)S(1)}, s32[]{:T(128)}, s32[]{:T(128)}) while((s32[]{:T(128)}, f32[128,128]{1,0:T(8,128)S(1)}, f32[128,128]{0,1:T(8,128)S(1)}, s32[]{:T(128)}, s32[]{:T(128)}) %tuple.200), condition=%wide.region_5.6_spmd.clone.clone, body=%wide.region_3.5_spmd.clone.clone.sunk | while | flops 197761 | bytes 71765 | solution.py:38
  142.6 0.8 fusion.125
  144.5 0.8 fusion.125
  146.6 0.8 fusion.125
  148.6 0.8 fusion.125
  150.6 0.8 fusion.125
  152.6 0.8 fusion.125
  154.6 0.8 fusion.125
  156.7 0.8 fusion.125
  158.7 0.8 fusion.125
  160.7 0.8 fusion.125
  402.0 5.1 convolution_bitcast_fusion.7
  407.9 41.0 %all-reduce.1 = (f32[128,16]{0,1:T(8,128)S(1)}, f32[16,16]{1,0:T(8,128)S(1)}) all-reduce(f32[128,16]{0,1:T(8,128)S(1)} %convolution_bitcast_fusion.7, f32[16,16]{1,0:T(8,128)S(1)} %fusion.63), channel_id=1, replica_groups=mesh['grp'=4,'row'=8] {'grp','row'}, use_global_device_ids=true, to_apply=%region_1.2 | all-reduce | flops 2304 | bytes 18432 | tf_op jit(solution)/shard_map/psum | solution.py:98
  449.0 186.3 %while.71 = (s32[]{:T(128)}, f32[128,16]{1,0:T(8,128)S(1)}, f32[128,16]{1,0:T(8,128)S(1)}, f32[128,128]{1,0:T(8,128)S(1)}, s32[]{:T(128)}, /*index=5*/s32[]{:T(128)}) while((s32[]{:T(128)}, f32[128,16]{1,0:T(8,128)S(1)}, f32[128,16]{1,0:T(8,128)S(1)}, f32[128,128]{1,0:T(8,128)S(1)}, s32[]{:T(128)}, /*index=5*/s32[]{:T(128)}) %tuple.203), condition=%wide.region_8.9_spmd, body=%wide.region_6.8_spmd.sunk | while | flops 24993 | bytes 69901 | solution.py:51
  635.3 187.1 %while.72 = (s32[]{:T(128)}, f32[128,16]{1,0:T(8,128)S(1)}, f32[128,16]{1,0:T(8,128)S(1)}, f32[128,128]{0,1:T(8,128)S(1)}, s32[]{:T(128)}, /*index=5*/s32[]{:T(128)}, s32[]{:T(128)}, s32[]{:T(128)}) while((s32[]{:T(128)}, f32[128,16]{1,0:T(8,128)S(1)}, f32[128,16]{1,0:T(8,128)S(1)}, f32[128,128]{0,1:T(8,128)S(1)}, s32[]{:T(128)}, ...), condition=%wide.region_11.12_spmd, body=%wide.region_9.11_spmd.sunk | while | flops 24997 | bytes 68439 | solution.py:65
  822.6 3.8 convolution_subtract_fusion
  827.2 26.0 %while.75 = (s32[]{:T(128)}, f32[16,16]{1,0:T(8,128)S(1)}, f32[16,16]{0,1:T(8,128)S(1)}, s32[]{:T(128)}, s32[]{:T(128)}) while((s32[]{:T(128)}, f32[16,16]{1,0:T(8,128)S(1)}, f32[16,16]{0,1:T(8,128)S(1)}, s32[]{:T(128)}, s32[]{:T(128)}) %tuple.209), condition=%wide.region_14.15_spmd.clone.clone, body=%wide.region_12.14_spmd.clone.clone.sunk | while | flops 3217 | bytes 11285 | solution.py:38
  853.2 22.8 %while.73 = (s32[]{:T(128)}, f32[16,16]{1,0:T(8,128)S(1)}, f32[16,16]{1,0:T(8,128)S(1)}, f32[16,16]{1,0:T(8,128)S(1)}, s32[]{:T(128)}, /*index=5*/s32[]{:T(128)}) while((s32[]{:T(128)}, f32[16,16]{1,0:T(8,128)S(1)}, f32[16,16]{1,0:T(8,128)S(1)}, f32[16,16]{1,0:T(8,128)S(1)}, s32[]{:T(128)}, /*index=5*/s32[]{:T(128)}) %tuple.212), condition=%wide.region_17.18_spmd, body=%wide.region_15.17_spmd.sunk | while | flops 3153 | bytes 12109 | solution.py:51
  876.6 1.3 collective-permute-start
  877.9 1.5 collective-permute-start.1
  881.4 4.0 copy.81
  885.3 30.5 %gather_fusion = f32[8192,16]{1,0:T(8,128)} fusion(f32[16,12288]{0,1:T(8,128)} %copy.81, s32[8192]{0:T(1024)S(1)} %fusion.44), kind=kCustom, calls=%fused_computation.clone | custom fusion | bytes 1081344 | tf_op jit(solution)/shard_map/jit(_take)/gather | solution.py:76
  915.8 2.8 copy.82
  918.6 30.5 %gather_fusion.1 = f32[8192,16]{1,0:T(8,128)} fusion(f32[16,12288]{0,1:T(8,128)} %copy.81, s32[8192]{0:T(1024)S(1)} %fusion.45), kind=kCustom, calls=%fused_computation.1.clone | custom fusion | bytes 1081344 | tf_op jit(solution)/shard_map/jit(_take)/gather | solution.py:76
  949.1 2.8 copy.84
  951.9 30.5 %gather_fusion.2 = f32[8192,16]{1,0:T(8,128)} fusion(f32[16,12288]{0,1:T(8,128)} %copy.81, s32[8192]{0:T(1024)S(1)} %fusion.46), kind=kCustom, calls=%fused_computation.2.clone | custom fusion | bytes 1081344 | tf_op jit(solution)/shard_map/jit(_take)/gather | solution.py:76
  982.3 2.8 copy.86
  985.1 30.5 %gather_fusion.3 = f32[8192,16]{1,0:T(8,128)} fusion(f32[16,12288]{0,1:T(8,128)} %copy.81, s32[8192]{0:T(1024)S(1)} %fusion.47), kind=kCustom, calls=%fused_computation.3.clone | custom fusion | bytes 1081344 | tf_op jit(solution)/shard_map/jit(_take)/gather | solution.py:76
  1015.6 3.5 copy.88
  1019.1 30.5 %gather_fusion.4 = f32[8192,16]{1,0:T(8,128)} fusion(f32[16,12288]{0,1:T(8,128)} %copy.81, s32[8192]{0:T(1024)S(1)} %fusion.48), kind=kCustom, calls=%fused_computation.4.clone | custom fusion | bytes 1081344 | tf_op jit(solution)/shard_map/jit(_take)/gather | solution.py:76
  1049.6 3.5 copy.90
  1053.1 30.5 %gather_fusion.5 = f32[8192,16]{1,0:T(8,128)} fusion(f32[16,12288]{0,1:T(8,128)} %copy.81, s32[8192]{0:T(1024)S(1)} %fusion.49), kind=kCustom, calls=%fused_computation.5.clone | custom fusion | bytes 1081344 | tf_op jit(solution)/shard_map/jit(_take)/gather | solution.py:76
  1083.5 3.5 copy.92
  1087.0 30.5 %gather_fusion.6 = f32[8192,16]{1,0:T(8,128)} fusion(f32[16,12288]{0,1:T(8,128)} %copy.81, s32[8192]{0:T(1024)S(1)} %fusion.50), kind=kCustom, calls=%fused_computation.6.clone | custom fusion | bytes 1081344 | tf_op jit(solution)/shard_map/jit(_take)/gather | solution.py:76
  1117.5 3.5 copy.94
  1121.0 30.5 %gather_fusion.7 = f32[8192,16]{1,0:T(8,128)} fusion(f32[16,12288]{0,1:T(8,128)} %copy.81, s32[8192]{0:T(1024)S(1)} %fusion.51), kind=kCustom, calls=%fused_computation.7.clone | custom fusion | bytes 1081344 | tf_op jit(solution)/shard_map/jit(_take)/gather | solution.py:76
  1151.5 3.5 copy.96
  1155.0 3.5 multiply_reduce_fusion
  1159.3 3.3 convolution_bitcast_fusion.6
  1163.4 3.4 convolution_bitcast_fusion.5
  1166.9 47.8 %all-reduce = (f32[2,144,16]{1,2,0:T(8,128)S(1)}, f32[16]{0:T(128)S(1)}) all-reduce(f32[2,144,16]{1,2,0:T(8,128)S(1)} %pad_maximum_fusion.2, f32[16]{0:T(128)S(1)} %copy-done.7), channel_id=1, replica_groups=mesh['grp'=4,'row'=8] {'grp','row'}, use_global_device_ids=true, to_apply=%region_18.20 | all-reduce | flops 4624 | bytes 36992 | tf_op jit(solution)/shard_map/psum | solution.py:127
  1215.8 1.0 pad_maximum_fusion
  (1453 shorter events, 572.8 us)
Async XLA Ops:
  9.3 392.1 %all-to-all-start = ((f32[4,4,8192]{2,0,1:T(4,128)}), f32[4,4,8192]{2,0,1:T(4,128)S(1)}, u32[]{:S(2)}, u32[]{:S(2)}) async-start(f32[4,4,8192]{2,0,1:T(4,128)} %copy.74), calls=%async_computation | async-start | bytes 1048576 | tf_op jit(solution)/shard_map/all_to_all | solution.py:90
  14.5 7.7 copy-start.3
  14.5 10.0 copy-start.2
  14.5 127.1 %all-reduce.4.cloned.1.call-start = ((), (), s32[]{:S(2)}) async-start(), calls=%async_computation.1 | async-start | bytes 131072 | tf_op jit(solution)/shard_map/psum | solution.py:96
  22.2 379.4 %copy-start.8 = (s32[16]{0:T(128)S(1)}, s32[16]{0:T(128)}, u32[]{:S(2)}) copy-start(s32[16]{0:T(128)} %param.20) | copy-start | bytes 196
  407.1 419.5 %copy-start.4 = (f32[128,128]{1,0:T(8,128)S(1)}, f32[128,128]{1,0:T(8,128)}, u32[]{:S(2)}) copy-start(f32[128,128]{1,0:T(8,128)} %all-reduce.4.cloned.1.call-done) | copy-start | bytes 196612
  635.3 244.1 %copy-start.9 = (s32[16]{0:T(128)S(1)}, s32[16]{0:T(128)}, u32[]{:S(2)}) copy-start(s32[16]{0:T(128)} %param.21) | copy-start | bytes 196
  876.6 286.1 %copy-start.1 = (f32[16,8192]{1,0:T(8,128)}, f32[16,8192]{1,0:T(8,128)S(1)}, u32[]{:S(2)}) copy-start(f32[16,8192]{1,0:T(8,128)S(1)} %fusion.65) | copy-start | bytes 1572868
  876.6 4.7 collective-permute-start
  877.9 3.4 collective-permute-start.1
  1121.0 34.0 %copy-start.5 = (f32[1,1,8192]{2,1,0:T(1,128)S(1)}, f32[1,1,8192]{2,1,0:T(1,128)}, u32[]{:S(2)}) copy-start(f32[1,1,8192]{2,1,0:T(1,128)} %get-tuple-element.621) | copy-start | bytes 98308
  1121.0 34.0 %copy-start.6 = (f32[1,1,8192]{2,1,0:T(1,128)S(1)}, f32[1,1,8192]{2,1,0:T(1,128)}, u32[]{:S(2)}) copy-start(f32[1,1,8192]{2,1,0:T(1,128)} %get-tuple-element.622) | copy-start | bytes 98308
  1155.0 4.3 copy-start
  1159.3 7.6 copy-start.7
Sparse Core Ops, SparseCore 0:
  22.3 119.2 all-reduce.3
where the time goes:
time: 1230 us; the launch traced here: 1220 us
  matrix products  361 us (29%)
  local copies, waits for them, and re-layouts  350 us (28%)
  other arithmetic  175 us (14%)
  waiting for transfers between devices  116 us (9%)
  loops' own time  110 us (9%)
  blocking collectives  88.8 us (7%)
  between operations  14.4 us (1%)
    gather x16, local copies, waits for them, and re-layouts, apply_local(): picked = jnp.take(extended, positions + offsets[slot_index], axis=1)  270 us
    dot_general x144, matrix products, cholesky_step(): jnp.dot(factor, factor_row, precision=lax.Precision.HIGHEST)  117 us
    psum x1, waiting for transfers between devices, body(): lax.psum(jnp.dot(basis, basis.T, precision=highest), ('grp', 'row'))  116 us
    dot_general x144, matrix products, forward_step(): jnp.dot(lower_row, solved, precision=lax.Precision.HIGHEST)  115 us
    another operation x2, loops' own time, cholesky_lower(): lax.fori_loop(0, order, cholesky_step, jnp.zeros(matrix.shape, matrix.dty...  104 us
    dot_general x128, matrix products, backward_step(): jnp.dot(upper_row, solved, precision=lax.Precision.HIGHEST)  102 us
    reduce_sum x144, other arithmetic, forward_step(): jnp.sum(jnp.where(jnp.arange(order, dtype=jnp.int32) == row_index, lower_...  87.3 us
    reduce_sum x128, other arithmetic, backward_step(): jnp.sum(jnp.where(jnp.arange(order, dtype=jnp.int32) == row_index, upper_...  77.7 us
  transfers between devices with their start and end apart: 4, of which 2 were waited for; matrix products, arithmetic and copies ran while one was open for 15% of the time, Pallas kernels for 0%

commit v1 on v0

v1 whole, which is shorter than its diff:
```python
import functools

import jax
import jax.numpy as jnp
from jax import lax
from jax.experimental import pallas as pl
from jax.experimental.pallas import tpu as pltpu
from jax.sharding import PartitionSpec as P

NPARAM = 64
HALO_BLOCKS = 16
F32 = jnp.float32
BF16 = jnp.bfloat16
MESH = pl.DeviceIdType.MESH
NT = (((1,), (1,)), ((), ()))
NN = (((1,), (0,)), ((), ()))


def split(x):
    high = x.astype(BF16)
    low = (x - high.astype(F32)).astype(BF16)
    return high, low


def bdot(a, b, dims):
    return lax.dot_general(a, b, dims, preferred_element_type=F32)


def hdot(a, b, dims=NN):
    return lax.dot_general(a, b, dims, precision=lax.Precision.HIGHEST, preferred_element_type=F32)


def gram_kernel(basis_ref, arrived_ref, out_ref, bb, ab, aa):
    step = pl.program_id(0)

    @pl.when(step == 0)
    def _():
        bb[...] = jnp.zeros_like(bb)
        ab[...] = jnp.zeros_like(ab)
        aa[...] = jnp.zeros_like(aa)

    x = jnp.concatenate(split(basis_ref[...]), axis=0)
    y = jnp.concatenate(split(arrived_ref[...]), axis=0)
    bb[...] += bdot(x, x, NT)
    ab[...] += bdot(y, x, NT)
    aa[...] += bdot(y, y, NT)

    @pl.when(step == pl.num_programs(0) - 1)
    def _():
        nb, ns = basis_ref.shape[0], arrived_ref.shape[0]
        g = bb[...]
        out_ref[0:nb, :] = (g[:nb, :nb] + g[nb:, nb:]) + (g[:nb, nb:] + g[nb:, :nb])
        c = ab[...]
        out_ref[nb : nb + ns, :] = (c[:ns, :nb] + c[ns:, nb:]) + (c[:ns, nb:] + c[ns:, :nb])
        s = aa[...]
        out_ref[nb + ns :, :] = jnp.zeros((ns, nb), F32)
        out_ref[nb + ns :, 0:ns] = (s[:ns, :ns] + s[ns:, ns:]) + (s[:ns, ns:] + s[ns:, :ns])


def gram_sums(basis, arrived, chunk):
    nb, rows = basis.shape
    ns = arrived.shape[0]
    return pl.pallas_call(
        gram_kernel,
        grid=(rows // chunk,),
        in_specs=[
            pl.BlockSpec((nb, chunk), lambda i: (0, i)),
            pl.BlockSpec((ns, chunk), lambda i: (0, i)),
        ],
        out_specs=pl.BlockSpec((nb + 2 * ns, nb), lambda i: (0, 0)),
        out_shape=jax.ShapeDtypeStruct((nb + 2 * ns, nb), F32),
        scratch_shapes=[
            pltpu.VMEM((2 * nb, 2 * nb), F32),
            pltpu.VMEM((2 * ns, 2 * nb), F32),
            pltpu.VMEM((2 * ns, 2 * ns), F32),
        ],
        compiler_params=pltpu.CompilerParams(vmem_limit_bytes=32 << 20),
        name="gram_sums",
    )(basis, arrived)


def reduce_kernel(n_row, count, x_ref, out_ref, held, send1, recv1, send2, recv2):
    tiles = x_ref.shape[0]
    stride = count // tiles
    me = lax.axis_index("grp") * n_row + lax.axis_index("row")
    mine = me // stride
    owner = jnp.logical_and(me == mine * stride, mine < tiles)

    def where(device):
        return (device // n_row, lax.rem(device, n_row))

    barrier = pltpu.get_barrier_semaphore()

    def greet(k, carry):
        pl.semaphore_signal(
            barrier, inc=1, device_id=where(lax.rem(me + k, count)), device_id_type=MESH
        )
        return carry

    lax.fori_loop(1, count, greet, 0)
    pl.semaphore_wait(barrier, count - 1)

    def first(tile):
        return pltpu.make_async_remote_copy(
            src_ref=x_ref.at[tile],
            dst_ref=held.at[me],
            send_sem=send1.at[tile],
            recv_sem=recv1.at[me],
            device_id=where(tile * stride),
            device_id_type=MESH,
        )

    def send_first(k, carry):
        tile = lax.rem(mine + k, tiles)

        @pl.when(tile * stride != me)
        def _():
            first(tile).start()

        return carry

    lax.fori_loop(0, tiles, send_first, 0)

    def second(device):
        return pltpu.make_async_remote_copy(
            src_ref=out_ref.at[mine],
            dst_ref=out_ref.at[mine],
            send_sem=send2.at[device],
            recv_sem=recv2.at[mine],
            device_id=where(device),
            device_id_type=MESH,
        )

    @pl.when(owner)
    def _():
        held[me] = x_ref[mine]

        def landed(k, carry):
            source = lax.rem(me + k, count)
            pltpu.make_async_remote_copy(
                src_ref=x_ref.at[mine],
                dst_ref=held.at[source],
                send_sem=send1.at[mine],
                recv_sem=recv1.at[source],
                device_id=where(source),
                device_id_type=MESH,
            ).wait_recv()
            return carry

        lax.fori_loop(1, count, landed, 0)
        out_ref[mine] = jnp.sum(held[...], axis=0)

        def send_second(k, carry):
            second(lax.rem(me + k, count)).start()
            return carry

        lax.fori_loop(1, count, send_second, 0)

    def finish(tile, carry):
        @pl.when(tile * stride != me)
        def _():
            first(tile).wait_send()
            pltpu.make_async_remote_copy(
                src_ref=out_ref.at[tile],
                dst_ref=out_ref.at[tile],
                send_sem=send2.at[0],
                recv_sem=recv2.at[tile],
                device_id=where(tile * stride),
                device_id_type=MESH,
            ).wait_recv()

        return carry

    lax.fori_loop(0, tiles, finish, 0)

    @pl.when(owner)
    def _():
        def sent(k, carry):
            second(lax.rem(me + k, count)).wait_send()
            return carry

        lax.fori_loop(1, count, sent, 0)


def reduce_tiles(x, ident):
    tiles = x.shape[0]
    n_row = lax.axis_size("row")
    count = lax.axis_size("grp") * n_row
    return pl.pallas_call(
        functools.partial(reduce_kernel, n_row, count),
        in_specs=[pl.BlockSpec(memory_space=pltpu.VMEM)],
        out_specs=pl.BlockSpec(memory_space=pltpu.VMEM),
        out_shape=jax.ShapeDtypeStruct(x.shape, F32),
        scratch_shapes=[
            pltpu.VMEM((count, 8, 128), F32),
            pltpu.SemaphoreType.DMA((tiles,)),
            pltpu.SemaphoreType.DMA((count,)),
            pltpu.SemaphoreType.DMA((count,)),
            pltpu.SemaphoreType.DMA((tiles,)),
        ],
        compiler_params=pltpu.CompilerParams(collective_id=ident, has_side_effects=True),
        name="reduce_tiles",
    )(x)


def factor_kernel(total, sums_ref, assign_ref, basis_ref, arrived_ref, new_ref, coords_ref, r_ref, m, wb, wa):
    nb = basis_ref.shape[0]
    ns = arrived_ref.shape[0]

    @pl.when(pl.program_id(0) == 0)
    def _():
        scale = 1.0 / total
        placing = (
            lax.broadcasted_iota(jnp.int32, (ns, ns), 0) == assign_ref[...]
        ).astype(F32)
        project = hdot(placing, sums_ref[nb : nb + ns, :] * scale)
        snap = hdot(hdot(placing, sums_ref[nb + ns :, 0:ns] * scale), placing, NT)
        m[0:nb, :] = sums_ref[0:nb, :] * scale
        m[nb : nb + ns, :] = project
        lanes = lax.broadcasted_iota(jnp.int32, (1, nb), 1)
        for k in range(nb):
            block = m[...]
            here = lanes == k
            row = block[k : k + 1, :]
            inv = 1.0 / row[:, k : k + 1]
            row = jnp.where(here, inv, row * inv)
            column = block[:, k : k + 1]
            m[...] = jnp.where(here, 0.0, block) - column * row
            m[k : k + 1, :] = row
        coords = -m[nb : nb + ns, :]
        coords_ref[...] = coords
        schur = snap - hdot(project, coords, NT)
        schur = 0.5 * (schur + hdot_transpose(schur))
        rows = lax.broadcasted_iota(jnp.int32, (ns, ns), 0)
        cols = lax.broadcasted_iota(jnp.int32, (ns, ns), 1)
        left = schur
        right = (rows == cols).astype(F32)
        below = lax.broadcasted_iota(jnp.int32, (ns, 1), 0)
        for k in range(ns):
            factor = left[:, k : k + 1] / left[k : k + 1, k : k + 1]
            factor = jnp.where(below > k, factor, 0.0)
            left, right = left - factor * left[k : k + 1, :], right - factor * right[k : k + 1, :]
        diagonal = jnp.sum(jnp.where(rows == cols, left, 0.0), axis=1, keepdims=True)
        root = 1.0 / jnp.sqrt(diagonal)
        r_ref[...] = jnp.where(cols >= rows, left * root, 0.0)
        inverse = right * root
        wb[...] = -hdot(inverse, coords)
        wa[...] = hdot(inverse, placing)

    bw = jnp.concatenate(split(wb[...]), axis=0)
    aw = jnp.concatenate(split(wa[...]), axis=0)
    bh, bl = split(basis_ref[...])
    ah, al = split(arrived_ref[...])
    out = (bdot(bw, bl, NN) + bdot(aw, al, NN)) + (bdot(bw, bh, NN) + bdot(aw, ah, NN))
    new_ref[...] = out[:ns] + out[ns:]


def hdot_transpose(x):
    n = x.shape[0]
    eye = (
        lax.broadcasted_iota(jnp.int32, (n, n), 0) == lax.broadcasted_iota(jnp.int32, (n, n), 1)
    ).astype(F32)
    return hdot(eye, x, NT)


def factor_and_columns(sums, assignment, basis, arrived, total, chunk):
    nb, rows = basis.shape
    ns = arrived.shape[0]
    whole = lambda i: (0, 0)
    return pl.pallas_call(
        functools.partial(factor_kernel, float(total)),
        grid=(rows // chunk,),
        in_specs=[
            pl.BlockSpec((nb + 2 * ns, nb), whole),
            pl.BlockSpec((1, ns), whole),
            pl.BlockSpec((nb, chunk), lambda i: (0, i)),
            pl.BlockSpec((ns, chunk), lambda i: (0, i)),
        ],
        out_specs=[
            pl.BlockSpec((ns, chunk), lambda i: (0, i)),
            pl.BlockSpec((ns, nb), whole),
            pl.BlockSpec((ns, ns), whole),
        ],
        out_shape=[
            jax.ShapeDtypeStruct((ns, rows), F32),
            jax.ShapeDtypeStruct((ns, nb), F32),
            jax.ShapeDtypeStruct((ns, ns), F32),
        ],
        scratch_shapes=[
            pltpu.VMEM((nb + ns, nb), F32),
            pltpu.VMEM((ns, nb), F32),
            pltpu.VMEM((ns, ns), F32),
        ],
        compiler_params=pltpu.CompilerParams(vmem_limit_bytes=32 << 20),
        name="factor_and_columns",
    )(sums, assignment.reshape(1, ns), basis, arrived)


def apply_kernel(low_ref, mid_ref, high_ref, visc_ref, off_ref, coef_ref, basis_ref, applied_ref, out_ref, ext, bx, nx, sq):
    step = pl.program_id(0)
    ns, chunk = 16, basis_ref.shape[1]
    nb = basis_ref.shape[0]
    terms, slots = coef_ref.shape[0], coef_ref.shape[1]
    width = low_ref.shape[1] // 128
    count = mid_ref.shape[1] // 128
    per_step = chunk // 128

    @pl.when(step == 0)
    def _():
        for b in range(width):
            ext[b] = low_ref[:, b * 128 : (b + 1) * 128]
            ext[width + count + b] = high_ref[:, b * 128 : (b + 1) * 128]
        for b in range(count):
            ext[width + b] = mid_ref[:, b * 128 : (b + 1) * 128]
        bx[...] = jnp.zeros_like(bx)
        nx[...] = jnp.zeros_like(nx)
        sq[...] = jnp.zeros_like(sq)

    lanes = lax.broadcasted_iota(jnp.int32, (slots, 128), 1)

    def one(c, carry):
        first = step * per_step + c
        at = pl.ds(pl.multiple_of(c * 128, 128), 128)
        spot = off_ref[:, at] + (lanes + width * 128)
        low_index = lax.bitwise_and(spot, 127)
        block_index = lax.shift_right_logical(spot, 7)
        totals = [[jnp.zeros((8, 128), F32) for h in range(ns // 8)] for k in range(terms)]
        for t in range(slots):
            lane = jnp.broadcast_to(low_index[t : t + 1, :], (8, 128))
            block = jnp.broadcast_to(block_index[t : t + 1, :], (8, 128))
            picked = [jnp.zeros((8, 128), F32) for h in range(ns // 8)]
            for b in range(2 * width + 1):
                same = block == b
                for h in range(ns // 8):
                    source = ext[first + b, h * 8 : (h + 1) * 8, :]
                    got = jnp.take_along_axis(source, lane, axis=1, mode="promise_in_bounds")
                    picked[h] = jnp.where(same, got, picked[h])
            for k in range(terms):
                weight = coef_ref[k, t : t + 1, at]
                for h in range(ns // 8):
                    totals[k][h] = totals[k][h] + weight * picked[h]
        for k in range(terms):
            for h in range(ns // 8):
                applied_ref[k, h * 8 : (h + 1) * 8, at] = totals[k][h]
        return carry

    lax.fori_loop(0, per_step, one, 0)

    flat = jnp.concatenate([applied_ref[k] for k in range(terms)], axis=0)
    combined = applied_ref[0]
    power = visc_ref[...]
    for k in range(1, terms):
        combined = combined + power * applied_ref[k]
        power = power * visc_ref[...]
    sq[...] += jnp.sum(combined * combined, axis=1, keepdims=True)
    y = jnp.concatenate(split(flat), axis=0)
    x = jnp.concatenate(split(basis_ref[...]), axis=0)
    here = pl.ds(pl.multiple_of(step * chunk, chunk), chunk)
    z = jnp.concatenate(split(mid_ref[:, here]), axis=0)
    bx[...] += bdot(y, x, NT)
    nx[...] += bdot(y, z, NT)

    @pl.when(step == pl.num_programs(0) - 1)
    def _():
        f = terms * ns
        g = bx[...]
        out_ref[0:f, :] = (g[:f, :nb] + g[f:, nb:]) + (g[:f, nb:] + g[f:, :nb])
        s = nx[...]
        out_ref[f : 2 * f, :] = jnp.zeros((f, 128), F32)
        out_ref[f : 2 * f, 0:ns] = (s[:f, :ns] + s[f:, ns:]) + (s[:f, ns:] + s[f:, :ns])
        out_ref[f : f + ns, ns : ns + 1] = sq[...]


def apply_and_blocks(low, new, high, viscosity, offsets, coefs, basis, chunk):
    nb, rows = basis.shape
    ns = new.shape[0]
    terms, slots = coefs.shape[0], coefs.shape[1]
    width = low.shape[1]
    whole = lambda i: (0, 0)
    blocks = (rows + 2 * width) // 128
    return pl.pallas_call(
        apply_kernel,
        grid=(rows // chunk,),
        in_specs=[
            pl.BlockSpec((ns, width), whole),
            pl.BlockSpec((ns, rows), whole),
            pl.BlockSpec((ns, width), whole),
            pl.BlockSpec((ns, 1), whole),
            pl.BlockSpec((slots, chunk), lambda i: (0, i)),
            pl.BlockSpec((terms, slots, chunk), lambda i: (0, 0, i)),
            pl.BlockSpec((nb, chunk), lambda i: (0, i)),
        ],
        out_specs=[
            pl.BlockSpec((terms, ns, chunk), lambda i: (0, 0, i)),
            pl.BlockSpec((2 * terms * ns, nb), whole),
        ],
        out_shape=[
            jax.ShapeDtypeStruct((terms, ns, rows), F32),
            jax.ShapeDtypeStruct((2 * terms * ns, nb), F32),
        ],
        scratch_shapes=[
            pltpu.VMEM((blocks, ns, 128), F32),
            pltpu.VMEM((2 * terms * ns, 2 * nb), F32),
            pltpu.VMEM((2 * terms * ns, 2 * ns), F32),
            pltpu.VMEM((ns, 1), F32),
        ],
        compiler_params=pltpu.CompilerParams(vmem_limit_bytes=32 << 20),
        name="apply_and_blocks",
    )(low, new, high, viscosity, offsets, coefs, basis)


def body(snapshots, basis, assignment, param_index, offsets, coefs):
    ns = assignment.shape[0]
    nb, local = basis.shape
    terms = coefs.shape[0]
    devices = lax.axis_size("grp") * lax.axis_size("row")
    total = local * devices
    width = HALO_BLOCKS * 128
    received = lax.all_to_all(snapshots, "grp", split_axis=1, concat_axis=0, tiled=True)
    arrived = received.reshape(ns, local)
    sums = gram_sums(basis, arrived, 1024)
    sums = reduce_tiles(sums.reshape(-1, 8, nb), 1).reshape(sums.shape)
    new, coords_t, r_factor = factor_and_columns(sums, assignment, basis, arrived, total, 2048)
    forward = [(i, i + 1) for i in range(devices - 1)]
    backward = [(i + 1, i) for i in range(devices - 1)]
    low = lax.ppermute(new[:, local - width :], ("grp", "row"), forward)
    high = lax.ppermute(new[:, :width], ("grp", "row"), backward)
    viscosity = (0.5 + param_index.astype(F32) / NPARAM).reshape(ns, 1)
    applied, parts = apply_and_blocks(low, new, high, viscosity, offsets, coefs, basis, 1024)
    parts = reduce_tiles(parts.reshape(-1, 8, nb), 2).reshape(parts.shape) / total
    f = terms * ns
    blocks = jnp.concatenate([parts[:f], parts[f:, :ns]], axis=1).reshape(terms, ns, nb + ns)
    return (new, applied, coords_t.T, r_factor, blocks.transpose(0, 2, 1), parts[f : f + ns, ns])


def solution(mesh):
    return jax.shard_map(
        body,
        mesh=mesh,
        in_specs=(
            P("grp", None, "row"),
            P(None, ("grp", "row")),
            P(),
            P(),
            P(None, ("grp", "row")),
            P(None, None, ("grp", "row")),
        ),
        out_specs=(P(None, ("grp", "row")), P(None, None, ("grp", "row")), P(), P(), P(), P()),
        check_vma=False,
    )
```

time: 1230 us -> 142 us (0.12)
  matrix products: 361 us -> 0 us
  local copies, waits for them, and re-layouts: 350 us -> 13.1 us
  other arithmetic: 175 us -> 1.39 us
  waiting for transfers between devices: 116 us -> 0.85 us
  loops' own time: 110 us -> 0 us
  Pallas kernels: 0 us -> 108 us
  blocking collectives: 88.8 us -> 13.5 us
  between operations: 14.4 us -> 0.73 us
    dot_general x429 -> x0, matrix products: 361 us -> none  [the longest x144 117 us: cholesky_step(): jnp.dot(factor, factor_row, precision=lax.Precision.HIGHEST)]
    gather x16 -> x0, local copies, waits for them, and re-layouts: 270 us -> none  [apply_local(): picked = jnp.take(extended, positions + offsets[slot_index], axis=1)]
    reduce_sum x273 -> x0, other arithmetic: 168 us -> none  [the longest x144 87.3 us: forward_step(): jnp.sum(jnp.where(jnp.arange(order, dtype=jnp.int32) == row_index, lower_...]
    psum x1 -> x0, waiting for transfers between devices: 116 us -> none  [body(): lax.psum(jnp.dot(basis, basis.T, precision=highest), ('grp', 'row'))]
    another operation x5 -> x0, loops' own time: 110 us -> none  [the longest x2 104 us: cholesky_lower(): lax.fori_loop(0, order, cholesky_step, jnp.zeros(matrix.shape, matrix.dty...]
    pallas_call x0 -> x5, Pallas kernels: none -> 108 us  [the longest x1 48.3 us: apply_and_blocks(): pl.pallas_call(apply_kernel, grid=(rows // chunk,), in_specs=[pl.BlockSpe...]
    psum x2 -> x0, blocking collectives: 88.8 us -> none  [the longest x1 47.8 us: body(): lax.psum((jnp.stack(blocks), jnp.sum(combined * combined, axis=1)), ('grp...]
    dynamic_update_slice x416 -> x0, local copies, waits for them, and re-layouts: 55.5 us -> none  [the longest x144 47.2 us: cholesky_step(): lax.dynamic_update_slice_in_dim(factor, fresh[:, None], column_index, 1)]
  transfers between devices with their start and end apart: 4 -> 2, of which waited for: 2 -> 1; matrix products, arithmetic and copies ran while one was open for 15% -> 0% of each run, Pallas kernels for 0% -> 0%
where the time goes in v1:
time: 142 us; the launch traced here: 141 us
  Pallas kernels  108 us (76%)
  blocking collectives  13.5 us (10%)
  local copies, waits for them, and re-layouts  13.1 us (9%)
  starting transfers between devices  4.33 us (3%)
    pallas_call x1, Pallas kernels, apply_and_blocks(): pl.pallas_call(apply_kernel, grid=(rows // chunk,), in_specs=[pl.BlockSpe...  48.3 us
    pallas_call x2, Pallas kernels, reduce_tiles(): pl.pallas_call(functools.partial(reduce_kernel, n_row, count), in_specs=[...  39.1 us
    pallas_call x1, Pallas kernels, factor_and_columns(): pl.pallas_call(functools.partial(factor_kernel, float(total)), grid=(rows...  15.8 us
    all_to_all x1, blocking collectives, body(): lax.all_to_all(snapshots, 'grp', split_axis=1, concat_axis=0, tiled=True)  13.5 us
    unnamed x24, local copies, waits for them, and re-layouts  11.7 us
    pallas_call x1, Pallas kernels, gram_sums(): pl.pallas_call(gram_kernel, grid=(rows // chunk,), in_specs=[pl.BlockSpec...  4.27 us
    ppermute x1, starting transfers between devices, body(): low = lax.ppermute(new[:, local - width:], ('grp', 'row'), forward)  3.04 us
  transfers between devices with their start and end apart: 2, of which 1 were waited for; matrix products, arithmetic and copies ran while one was open for 0% of the time, Pallas kernels for 0%

profile of v1, /device:TPU:0, one launch (start us, length us, event | category | flops | bytes accessed | tf_op | source)
XLA Modules:
  0.0 141.4 jit_solution(15668171660966183284)
XLA Ops:
  0.6 0.0 copy-start.9
  0.6 1.4 copy.15
  2.0 13.5 %all_to_all.15 = f32[4,4,8192]{2,0,1:T(4,128)S(1)} all-to-all(f32[4,4,8192]{2,0,1:T(4,128)S(1)} %copy.15), channel_id=1, replica_groups=mesh['grp'=4,'row'=8] {'grp'}, dimensions={1} | all-to-all | bytes 1048576 | tf_op jit(solution)/shard_map/all_to_all | solution.py:419
  15.5 0.2 reshape.38.arrived_ref
  15.7 0.0 copy-start
  15.7 2.2 %copy-done = f32[128,8192]{1,0:T(8,128)S(1)} copy-done((f32[128,8192]{1,0:T(8,128)S(1)}, f32[128,8192]{1,0:T(8,128)}, u32[]{:S(2)}) %copy-start) | copy-done | bytes 4194328
  17.9 0.0 copy-start.10
  17.9 0.0 copy-start.4
  17.9 0.0 copy-start.7
  17.9 4.3 %gram_sums.1 = f32[160,128]{1,0:T(8,128)S(1)} custom-call(f32[128,8192]{1,0:T(8,128)S(1)} %copy-done, f32[16,8192]{1,0:T(8,128)S(1)} %reshape.38.arrived_ref), custom_call_target="tpu_custom_call" | custom-call | tf_op jit(solution)/shard_map/gram_sums/pallas_call | solution.py:63
  22.2 0.0 copy-start.6
  22.2 0.6 copy-done.6
  22.8 17.4 %reduce_tiles.2 = f32[20,8,128]{2,1,0:T(8,128)} custom-call(f32[20,8,128]{2,1,0:T(8,128)} %bitcast.21), custom_call_target="tpu_custom_call" | custom-call | tf_op jit(solution)/shard_map/reduce_tiles/pallas_call | solution.py:189
  40.2 0.0 copy-done.9
  40.2 0.0 copy-start.1
  40.2 2.2 %copy-done.1 = f32[128,8192]{1,0:T(8,128)S(1)} copy-done((f32[128,8192]{1,0:T(8,128)S(1)}, f32[128,8192]{1,0:T(8,128)}, u32[]{:S(2)}) %copy-start.1) | copy-done | bytes 4194328
  42.4 0.0 copy-start.5
  42.4 0.9 copy-done.5
  43.3 15.8 %factor_and_columns.1 = (f32[16,8192]{1,0:T(8,128)}, f32[16,128]{1,0:T(8,128)}, f32[16,16]{1,0:T(8,128)}) custom-call(f32[160,128]{1,0:T(8,128)S(1)} %bitcast.20, s32[1,16]{1,0:T(1,128)S(1)} %bitcast.23, f32[128,8192]{1,0:T(8,128)S(1)} %copy-done.1, f32[16,8192]{1,0:T(8,128)S(1)} %reshape.38.arrived_ref), custom_call_target="tpu_custom_call" | custom-call | tf_op jit(solution)/shard_map/factor_and_columns/pallas_call | solution.py:270
  59.1 1.0 fusion.1
  60.1 1.3 collective-permute-start.1
  61.4 3.0 %collective-permute-start = (f32[16,2048]{1,0:T(8,128)S(1)}, f32[16,2048]{1,0:T(8,128)S(1)}, u32[]{:S(2)}, u32[]{:S(2)}) collective-permute-start(f32[16,2048]{1,0:T(8,128)S(1)} %get-tuple-element.17), channel_id=1, source_target_pairs={{0,1},{1,2},{2,3},{3,4},{4,5},{5,6},{6,7},{7,8},{8,9},{9,10},{10,1... | collective-permute-start | bytes 393224 | tf_op jit(solution)/shard_map/ppermute | solution.py:426
  64.4 0.0 copy-done.10
  64.5 0.1 copy.16.visc_ref
  64.5 0.0 collective-permute-done.1.high_ref
  64.5 0.9 collective-permute-done.low_ref
  65.4 0.0 copy-done.4
  65.4 0.0 copy-done.7
  65.4 0.0 copy-start.2
  65.4 2.2 %copy-done.2 = f32[128,8192]{1,0:T(8,128)S(1)} copy-done((f32[128,8192]{1,0:T(8,128)S(1)}, f32[128,8192]{1,0:T(8,128)}, u32[]{:S(2)}) %copy-start.2) | copy-done | bytes 4194328
  67.6 0.0 copy-start.3
  67.6 1.0 copy-done.3
  68.6 48.3 %apply_and_blocks.1 = (f32[2,16,8192]{2,1,0:T(8,128)}, f32[64,128]{1,0:T(8,128)S(1)}) custom-call(f32[16,2048]{1,0:T(8,128)S(1)} %collective-permute-done.low_ref, f32[16,8192]{1,0:T(8,128)S(1)} %copy-done.3, f32[16,2048]{1,0:T(8,128)S(1)} %collective-permute-done.1.high_ref, f32[16,1]{1,0:T(8,128)S(1)} %copy.16.visc_ref, s32[8,8192]{1,0:T(8,128)S(1)} %copy-done.7, ...), custom_call_target="tpu_custom_call" | custom-call | tf_op jit(solution)/shard_map/apply_and_blocks/pallas_call | solution.py:381
  117.0 0.0 copy-start.8
  117.0 0.6 copy-done.8
  117.6 21.8 %reduce_tiles.3 = f32[8,8,128]{2,1,0:T(8,128)} custom-call(f32[8,8,128]{2,1,0:T(8,128)} %bitcast.22), custom_call_target="tpu_custom_call" | custom-call | tf_op jit(solution)/shard_map/reduce_tiles/pallas_call | solution.py:189
  139.4 0.8 broadcast_multiply_fusion
  140.1 0.1 slice.26
  140.2 0.6 copy.18
  140.8 0.6 pad_maximum_fusion
  (3 shorter events, 0.0 us)
Async XLA Ops:
  0.6 39.5 %copy-start.9 = (s32[16]{0:T(128)S(1)}, s32[16]{0:T(128)}, u32[]{:S(2)}) copy-start(s32[16]{0:T(128)} %param.8) | copy-start | bytes 196
  15.7 2.2 %copy-start = (f32[128,8192]{1,0:T(8,128)S(1)}, f32[128,8192]{1,0:T(8,128)}, u32[]{:S(2)}) copy-start(f32[128,8192]{1,0:T(8,128)} %basis_ref.5) | copy-start | bytes 12582916
  17.9 46.5 %copy-start.10 = (s32[16]{0:T(128)S(1)}, s32[16]{0:T(128)}, u32[]{:S(2)}) copy-start(s32[16]{0:T(128)} %param.9) | copy-start | bytes 196
  17.9 47.5 %copy-start.4 = (f32[2,8,8192]{2,1,0:T(8,128)S(1)}, f32[2,8,8192]{2,1,0:T(8,128)}, u32[]{:S(2)}) copy-start(f32[2,8,8192]{2,1,0:T(8,128)} %coef_ref.1) | copy-start | bytes 1572868
  17.9 47.5 %copy-start.7 = (s32[8,8192]{1,0:T(8,128)S(1)}, s32[8,8192]{1,0:T(8,128)}, u32[]{:S(2)}) copy-start(s32[8,8192]{1,0:T(8,128)} %off_ref.1) | copy-start | bytes 786436
  22.2 0.6 copy-start.6
  40.2 2.2 %copy-start.1 = (f32[128,8192]{1,0:T(8,128)S(1)}, f32[128,8192]{1,0:T(8,128)}, u32[]{:S(2)}) copy-start(f32[128,8192]{1,0:T(8,128)} %basis_ref.5) | copy-start | bytes 12582916
  42.4 0.9 copy-start.5
  60.1 4.5 %collective-permute-start.1 = (f32[16,2048]{1,0:T(8,128)S(1)}, f32[16,2048]{1,0:T(8,128)S(1)}, u32[]{:S(2)}, u32[]{:S(2)}) collective-permute-start(f32[16,2048]{1,0:T(8,128)S(1)} %get-tuple-element.16), channel_id=1, source_target_pairs={{1,0},{2,1},{3,2},{4,3},{5,4},{6,5},{7,6},{8,7},{9,8},{10,9},{11,1... | collective-permute-start | bytes 393224 | tf_op jit(solution)/shard_map/ppermute | solution.py:427
  61.4 4.0 %collective-permute-start = (f32[16,2048]{1,0:T(8,128)S(1)}, f32[16,2048]{1,0:T(8,128)S(1)}, u32[]{:S(2)}, u32[]{:S(2)}) collective-permute-start(f32[16,2048]{1,0:T(8,128)S(1)} %get-tuple-element.17), channel_id=1, source_target_pairs={{0,1},{1,2},{2,3},{3,4},{4,5},{5,6},{6,7},{7,8},{8,9},{9,10},{10,1... | collective-permute-start | bytes 393224 | tf_op jit(solution)/shard_map/ppermute | solution.py:426
  65.4 2.2 %copy-start.2 = (f32[128,8192]{1,0:T(8,128)S(1)}, f32[128,8192]{1,0:T(8,128)}, u32[]{:S(2)}) copy-start(f32[128,8192]{1,0:T(8,128)} %basis_ref.5) | copy-start | bytes 12582916
  67.6 1.0 copy-start.3
  117.0 0.6 copy-start.8

commit v2 on v1

--- a/solution.py
+++ b/solution.py
@@ -53,13 +53,14 @@
         c = ab[...]
         out_ref[nb : nb + ns, :] = (c[:ns, :nb] + c[ns:, nb:]) + (c[:ns, nb:] + c[ns:, :nb])
         s = aa[...]
-        out_ref[nb + ns :, :] = jnp.zeros((ns, nb), F32)
-        out_ref[nb + ns :, 0:ns] = (s[:ns, :ns] + s[ns:, ns:]) + (s[:ns, ns:] + s[ns:, :ns])
+        out_ref[nb + ns :, :] = jnp.zeros((out_ref.shape[0] - nb - ns, nb), F32)
+        out_ref[nb + ns : nb + 2 * ns, 0:ns] = (s[:ns, :ns] + s[ns:, ns:]) + (s[:ns, ns:] + s[ns:, :ns])
 
 
 def gram_sums(basis, arrived, chunk):
     nb, rows = basis.shape
     ns = arrived.shape[0]
+    height = padded_rows(nb + 2 * ns)
     return pl.pallas_call(
         gram_kernel,
         grid=(rows // chunk,),
@@ -67,140 +68,251 @@
             pl.BlockSpec((nb, chunk), lambda i: (0, i)),
             pl.BlockSpec((ns, chunk), lambda i: (0, i)),
         ],
-        out_specs=pl.BlockSpec((nb + 2 * ns, nb), lambda i: (0, 0)),
-        out_shape=jax.ShapeDtypeStruct((nb + 2 * ns, nb), F32),
+        out_specs=pl.BlockSpec((height, nb), lambda i: (0, 0)),
+        out_shape=jax.ShapeDtypeStruct((height, nb), F32),
         scratch_shapes=[
             pltpu.VMEM((2 * nb, 2 * nb), F32),
             pltpu.VMEM((2 * ns, 2 * nb), F32),
             pltpu.VMEM((2 * ns, 2 * ns), F32),
         ],
-        compiler_params=pltpu.CompilerParams(vmem_limit_bytes=32 << 20),
+        compiler_params=pltpu.CompilerParams(vmem_limit_bytes=60 << 20),
         name="gram_sums",
     )(basis, arrived)
 
 
-def reduce_kernel(n_row, count, x_ref, out_ref, held, send1, recv1, send2, recv2):
-    tiles = x_ref.shape[0]
-    stride = count // tiles
+def exchange_kernel(n_grp, snap_ref, out_ref, ready, held, send_sem, recv_sem):
+    me = lax.axis_index("grp")
+    row = lax.axis_index("row")
+    own = snap_ref.shape[0]
+    barrier = pltpu.get_barrier_semaphore()
+    for k in range(1, n_grp):
+        pl.semaphore_signal(
+            barrier, inc=1, device_id=(lax.rem(me + k, n_grp), row), device_id_type=MESH
+        )
+    for q in range(n_grp):
+        ready[q] = snap_ref[:, q, :]
+    pl.semaphore_wait(barrier, n_grp - 1)
+
+    def copy(k):
+        other = lax.rem(me + k, n_grp)
+        return pltpu.make_async_remote_copy(
+            src_ref=ready.at[other],
+            dst_ref=held.at[k],
+            send_sem=send_sem.at[k],
+            recv_sem=recv_sem.at[k],
+            device_id=(other, row),
+            device_id_type=MESH,
+        )
+
+    for k in range(1, n_grp):
+        copy(k).start()
+    held[0] = ready[me]
+    for k in range(1, n_grp):
+        copy(k).wait()
+    for q in range(n_grp):
+        out_ref[q * own : (q + 1) * own, :] = held[lax.rem(me - q + n_grp, n_grp)]
+
+
+def exchange(snapshots):
+    own, n_grp, local = snapshots.shape
+    return pl.pallas_call(
+        functools.partial(exchange_kernel, n_grp),
+        in_specs=[pl.BlockSpec(memory_space=pltpu.VMEM)],
+        out_specs=pl.BlockSpec(memory_space=pltpu.VMEM),
+        out_shape=jax.ShapeDtypeStruct((own * n_grp, local), F32),
+        scratch_shapes=[
+            pltpu.VMEM((n_grp, own, local), F32),
+            pltpu.VMEM((n_grp, own, local), F32),
+            pltpu.SemaphoreType.DMA((n_grp,)),
+            pltpu.SemaphoreType.DMA((n_grp,)),
+        ],
+        compiler_params=pltpu.CompilerParams(
+            collective_id=3, has_side_effects=True, vmem_limit_bytes=16 << 20
+        ),
+        name="exchange",
+    )(snapshots)
+
+
+def halo_kernel(n_row, count, new_ref, low_ref, high_ref, send_sem, recv_sem):
     me = lax.axis_index("grp") * n_row + lax.axis_index("row")
-    mine = me // stride
-    owner = jnp.logical_and(me == mine * stride, mine < tiles)
+    width = low_ref.shape[1]
+    local = new_ref.shape[1]
+    barrier = pltpu.get_barrier_semaphore()
 
     def where(device):
         return (device // n_row, lax.rem(device, n_row))
 
-    barrier = pltpu.get_barrier_semaphore()
-
-    def greet(k, carry):
+    has_left = me > 0
+    has_right = me < count - 1
+
+    for other in (me + 1, me + count - 1):
         pl.semaphore_signal(
-            barrier, inc=1, device_id=where(lax.rem(me + k, count)), device_id_type=MESH
-        )
-        return carry
-
-    lax.fori_loop(1, count, greet, 0)
-    pl.semaphore_wait(barrier, count - 1)
-
-    def first(tile):
+            barrier, inc=1, device_id=where(lax.rem(other, count)), device_id_type=MESH
+        )
+    pl.semaphore_wait(barrier, 2)
+
+    def right():
         return pltpu.make_async_remote_copy(
-            src_ref=x_ref.at[tile],
-            dst_ref=held.at[me],
-            send_sem=send1.at[tile],
-            recv_sem=recv1.at[me],
-            device_id=where(tile * stride),
+            src_ref=new_ref.at[:, local - width :],
+            dst_ref=low_ref,
+            send_sem=send_sem.at[0],
+            recv_sem=recv_sem.at[0],
+            device_id=where(me + 1),
             device_id_type=MESH,
         )
 
-    def send_first(k, carry):
-        tile = lax.rem(mine + k, tiles)
-
-        @pl.when(tile * stride != me)
-        def _():
-            first(tile).start()
-
-        return carry
-
-    lax.fori_loop(0, tiles, send_first, 0)
-
-    def second(device):
+    def left():
         return pltpu.make_async_remote_copy(
-            src_ref=out_ref.at[mine],
-            dst_ref=out_ref.at[mine],
-            send_sem=send2.at[device],
-            recv_sem=recv2.at[mine],
-            device_id=where(device),
+            src_ref=new_ref.at[:, 0:width],
+            dst_ref=high_ref,
+            send_sem=send_sem.at[1],
+            recv_sem=recv_sem.at[1],
+            device_id=where(me - 1),
             device_id_type=MESH,
         )
 
-    @pl.when(owner)
-    def _():
-        held[me] = x_ref[mine]
-
-        def landed(k, carry):
-            source = lax.rem(me + k, count)
-            pltpu.make_async_remote_copy(
-                src_ref=x_ref.at[mine],
-                dst_ref=held.at[source],
-                send_sem=send1.at[mine],
-                recv_sem=recv1.at[source],
-                device_id=where(source),
-                device_id_type=MESH,
-            ).wait_recv()
-            return carry
-
-        lax.fori_loop(1, count, landed, 0)
-        out_ref[mine] = jnp.sum(held[...], axis=0)
-
-        def send_second(k, carry):
-            second(lax.rem(me + k, count)).start()
-            return carry
-
-        lax.fori_loop(1, count, send_second, 0)
-
-    def finish(tile, carry):
-        @pl.when(tile * stride != me)
-        def _():
-            first(tile).wait_send()
-            pltpu.make_async_remote_copy(
-                src_ref=out_ref.at[tile],
-                dst_ref=out_ref.at[tile],
-                send_sem=send2.at[0],
-                recv_sem=recv2.at[tile],
-                device_id=where(tile * stride),
-                device_id_type=MESH,
-            ).wait_recv()
-
-        return carry
-
-    lax.fori_loop(0, tiles, finish, 0)
-
-    @pl.when(owner)
-    def _():
-        def sent(k, carry):
-            second(lax.rem(me + k, count)).wait_send()
-            return carry
-
-        lax.fori_loop(1, count, sent, 0)
-
-
-def reduce_tiles(x, ident):
-    tiles = x.shape[0]
+    @pl.when(has_right)
+    def _():
+        right().start()
+
+    @pl.when(has_left)
+    def _():
+        left().start()
+
+    @pl.when(jnp.logical_not(has_left))
+    def _():
+        low_ref[...] = jnp.zeros_like(low_ref)
+
+    @pl.when(jnp.logical_not(has_right))
+    def _():
+        high_ref[...] = jnp.zeros_like(high_ref)
+
+    @pl.when(has_right)
+    def _():
+        right().wait_send()
+        left().wait_recv()
+
+    @pl.when(has_left)
+    def _():
+        left().wait_send()
+        right().wait_recv()
+
+
+def halo(new, width):
     n_row = lax.axis_size("row")
     count = lax.axis_size("grp") * n_row
+    vmem = pl.BlockSpec(memory_space=pltpu.VMEM)
+    side = jax.ShapeDtypeStruct((new.shape[0], width), F32)
     return pl.pallas_call(
-        functools.partial(reduce_kernel, n_row, count),
+        functools.partial(halo_kernel, n_row, count),
+        in_specs=[vmem],
+        out_specs=[vmem, vmem],
+        out_shape=[side, side],
+        scratch_shapes=[pltpu.SemaphoreType.DMA((2,)), pltpu.SemaphoreType.DMA((2,))],
+        compiler_params=pltpu.CompilerParams(collective_id=4, has_side_effects=True),
+        name="halo",
+    )(new)
+
+
+def reduce_kernel(n_grp, n_row, x_ref, out_ref, held, summed, send1, recv1, send2, recv2, send3, recv3):
+    mg = lax.axis_index("grp")
+    mr = lax.axis_index("row")
+    barrier = pltpu.get_barrier_semaphore()
+
+    def greet_row(k, carry):
+        pl.semaphore_signal(
+            barrier, inc=1, device_id=(mg, lax.rem(mr + k, n_row)), device_id_type=MESH
+        )
+        return carry
+
+    lax.fori_loop(1, n_row, greet_row, 0)
+    for k in range(1, n_grp):
+        pl.semaphore_signal(
+            barrier, inc=1, device_id=(lax.rem(mg + k, n_grp), mr), device_id_type=MESH
+        )
+    pl.semaphore_wait(barrier, n_row + n_grp - 2)
+
+    def first(k):
+        other = lax.rem(mr + k, n_row)
+        return pltpu.make_async_remote_copy(
+            src_ref=x_ref.at[other],
+            dst_ref=held.at[k],
+            send_sem=send1.at[k],
+            recv_sem=recv1.at[k],
+            device_id=(mg, other),
+            device_id_type=MESH,
+        )
+
+    def second(k):
+        return pltpu.make_async_remote_copy(
+            src_ref=summed.at[0],
+            dst_ref=summed.at[k],
+            send_sem=send2.at[k],
+            recv_sem=recv2.at[k],
+            device_id=(lax.rem(mg + k, n_grp), mr),
+            device_id_type=MESH,
+        )
+
+    def third(k, block):
+        return pltpu.make_async_remote_copy(
+            src_ref=out_ref.at[block],
+            dst_ref=out_ref.at[block],
+            send_sem=send3.at[k],
+            recv_sem=recv3.at[k],
+            device_id=(mg, lax.rem(mr + k, n_row)),
+            device_id_type=MESH,
+        )
+
+    def run(low, high, act):
+        def one(k, carry):
+            act(k)
+            return carry
+
+        lax.fori_loop(low, high, one, 0)
+
+    run(1, n_row, lambda k: first(k).start())
+    held[0] = x_ref[mr]
+    run(1, n_row, lambda k: first(k).wait_recv())
+    summed[0] = jnp.sum(held[...], axis=0)
+    run(1, n_grp, lambda k: second(k).start())
+    run(1, n_grp, lambda k: second(k).wait())
+    total = summed[mg]
+    for q in range(1, n_grp):
+        total = total + summed[lax.rem(mg + n_grp - q, n_grp)]
+    out_ref[mr] = total
+    run(1, n_row, lambda k: third(k, mr).start())
+    run(1, n_row, lambda k: third(k, lax.rem(mr - k + n_row, n_row)).wait_recv())
+    run(1, n_row, lambda k: first(k).wait_send())
+    run(1, n_row, lambda k: third(k, mr).wait_send())
+
+
+def padded_rows(rows):
+    step = 8 * lax.axis_size("row")
+    return -(-rows // step) * step
+
+
+def reduce_tiles(x, ident):
+    n_row = lax.axis_size("row")
+    n_grp = lax.axis_size("grp")
+    shape = (n_row, x.shape[0] // n_row, x.shape[1])
+    return pl.pallas_call(
+        functools.partial(reduce_kernel, n_grp, n_row),
         in_specs=[pl.BlockSpec(memory_space=pltpu.VMEM)],
         out_specs=pl.BlockSpec(memory_space=pltpu.VMEM),
-        out_shape=jax.ShapeDtypeStruct(x.shape, F32),
+        out_shape=jax.ShapeDtypeStruct(shape, F32),
         scratch_shapes=[
-            pltpu.VMEM((count, 8, 128), F32),
-            pltpu.SemaphoreType.DMA((tiles,)),
-            pltpu.SemaphoreType.DMA((count,)),
-            pltpu.SemaphoreType.DMA((count,)),
-            pltpu.SemaphoreType.DMA((tiles,)),
+            pltpu.VMEM(shape, F32),
+            pltpu.VMEM((n_grp,) + shape[1:], F32),
+            pltpu.SemaphoreType.DMA((n_row,)),
+            pltpu.SemaphoreType.DMA((n_row,)),
+            pltpu.SemaphoreType.DMA((n_grp,)),
+            pltpu.SemaphoreType.DMA((n_grp,)),
+            pltpu.SemaphoreType.DMA((n_row,)),
+            pltpu.SemaphoreType.DMA((n_row,)),
         ],
         compiler_params=pltpu.CompilerParams(collective_id=ident, has_side_effects=True),
         name="reduce_tiles",
-    )(x)
+    )(x.reshape(shape)).reshape(x.shape)
 
 
 def factor_kernel(total, sums_ref, assign_ref, basis_ref, arrived_ref, new_ref, coords_ref, r_ref, m, wb, wa):
@@ -214,7 +326,7 @@
             lax.broadcasted_iota(jnp.int32, (ns, ns), 0) == assign_ref[...]
         ).astype(F32)
         project = hdot(placing, sums_ref[nb : nb + ns, :] * scale)
-        snap = hdot(hdot(placing, sums_ref[nb + ns :, 0:ns] * scale), placing, NT)
+        snap = hdot(hdot(placing, sums_ref[nb + ns : nb + 2 * ns, 0:ns] * scale), placing, NT)
         m[0:nb, :] = sums_ref[0:nb, :] * scale
         m[nb : nb + ns, :] = project
         lanes = lax.broadcasted_iota(jnp.int32, (1, nb), 1)
@@ -271,7 +383,7 @@
         functools.partial(factor_kernel, float(total)),
         grid=(rows // chunk,),
         in_specs=[
-            pl.BlockSpec((nb + 2 * ns, nb), whole),
+            pl.BlockSpec(sums.shape, whole),
             pl.BlockSpec((1, ns), whole),
             pl.BlockSpec((nb, chunk), lambda i: (0, i)),
             pl.BlockSpec((ns, chunk), lambda i: (0, i)),
@@ -291,7 +403,7 @@
             pltpu.VMEM((ns, nb), F32),
             pltpu.VMEM((ns, ns), F32),
         ],
-        compiler_params=pltpu.CompilerParams(vmem_limit_bytes=32 << 20),
+        compiler_params=pltpu.CompilerParams(vmem_limit_bytes=60 << 20),
         name="factor_and_columns",
     )(sums, assignment.reshape(1, ns), basis, arrived)
 
@@ -366,7 +478,7 @@
         g = bx[...]
         out_ref[0:f, :] = (g[:f, :nb] + g[f:, nb:]) + (g[:f, nb:] + g[f:, :nb])
         s = nx[...]
-        out_ref[f : 2 * f, :] = jnp.zeros((f, 128), F32)
+        out_ref[f:, :] = jnp.zeros((out_ref.shape[0] - f, nb), F32)
         out_ref[f : 2 * f, 0:ns] = (s[:f, :ns] + s[f:, ns:]) + (s[:f, ns:] + s[f:, :ns])
         out_ref[f : f + ns, ns : ns + 1] = sq[...]
 
@@ -378,6 +490,7 @@
     width = low.shape[1]
     whole = lambda i: (0, 0)
     blocks = (rows + 2 * width) // 128
+    height = padded_rows(2 * terms * ns)
     return pl.pallas_call(
         apply_kernel,
         grid=(rows // chunk,),
@@ -392,11 +505,11 @@
         ],
         out_specs=[
             pl.BlockSpec((terms, ns, chunk), lambda i: (0, 0, i)),
-            pl.BlockSpec((2 * terms * ns, nb), whole),
+            pl.BlockSpec((height, nb), whole),
         ],
         out_shape=[
             jax.ShapeDtypeStruct((terms, ns, rows), F32),
-            jax.ShapeDtypeStruct((2 * terms * ns, nb), F32),
+            jax.ShapeDtypeStruct((height, nb), F32),
         ],
         scratch_shapes=[
             pltpu.VMEM((blocks, ns, 128), F32),
@@ -404,7 +517,7 @@
             pltpu.VMEM((2 * terms * ns, 2 * ns), F32),
             pltpu.VMEM((ns, 1), F32),
         ],
-        compiler_params=pltpu.CompilerParams(vmem_limit_bytes=32 << 20),
+        compiler_params=pltpu.CompilerParams(vmem_limit_bytes=60 << 20),
         name="apply_and_blocks",
     )(low, new, high, viscosity, offsets, coefs, basis)
 
@@ -416,20 +529,15 @@
     devices = lax.axis_size("grp") * lax.axis_size("row")
     total = local * devices
     width = HALO_BLOCKS * 128
-    received = lax.all_to_all(snapshots, "grp", split_axis=1, concat_axis=0, tiled=True)
-    arrived = received.reshape(ns, local)
-    sums = gram_sums(basis, arrived, 1024)
-    sums = reduce_tiles(sums.reshape(-1, 8, nb), 1).reshape(sums.shape)
+    arrived = exchange(snapshots)
+    sums = reduce_tiles(gram_sums(basis, arrived, 1024), 1)
     new, coords_t, r_factor = factor_and_columns(sums, assignment, basis, arrived, total, 2048)
-    forward = [(i, i + 1) for i in range(devices - 1)]
-    backward = [(i + 1, i) for i in range(devices - 1)]
-    low = lax.ppermute(new[:, local - width :], ("grp", "row"), forward)
-    high = lax.ppermute(new[:, :width], ("grp", "row"), backward)
+    low, high = halo(new, width)
     viscosity = (0.5 + param_index.astype(F32) / NPARAM).reshape(ns, 1)
     applied, parts = apply_and_blocks(low, new, high, viscosity, offsets, coefs, basis, 1024)
-    parts = reduce_tiles(parts.reshape(-1, 8, nb), 2).reshape(parts.shape) / total
+    parts = reduce_tiles(parts, 2) / total
     f = terms * ns
-    blocks = jnp.concatenate([parts[:f], parts[f:, :ns]], axis=1).reshape(terms, ns, nb + ns)
+    blocks = jnp.concatenate([parts[:f], parts[f : 2 * f, :ns]], axis=1).reshape(terms, ns, nb + ns)
     return (new, applied, coords_t.T, r_factor, blocks.transpose(0, 2, 1), parts[f : f + ns, ns])
 
 

time: 142 us -> 132 us (0.930)
  Pallas kernels: 108 us -> 126 us
  blocking collectives: 13.5 us -> 0 us
  local copies, waits for them, and re-layouts: 13.1 us -> 3.17 us
  starting transfers between devices: 4.33 us -> 0 us
    all_to_all x1 -> x0, blocking collectives: 13.5 us -> none  [body(): lax.all_to_all(snapshots, 'grp', split_axis=1, concat_axis=0, tiled=True)]
    pallas_call x2 -> x4, Pallas kernels: 39.1 us -> 50.7 us  [the longest x2 35.4 us: reduce_tiles(): pl.pallas_call(functools.partial(reduce_kernel, n_grp, n_row), in_specs=[...]
    unnamed x24 -> x5, local copies, waits for them, and re-layouts: 11.7 us -> 2.41 us
    ppermute x2 -> x0, starting transfers between devices: 4.33 us -> none  [the longest x1 3.04 us: body(): low = lax.ppermute(new[:, local - width:], ('grp', 'row'), forward)]
    pallas_call x1, Pallas kernels: 4.27 us -> 7.45 us  [gram_sums(): pl.pallas_call(gram_kernel, grid=(rows // chunk,), in_specs=[pl.BlockSpec...]
    pallas_call x1, Pallas kernels: 15.8 us -> 17.8 us  [factor_and_columns(): pl.pallas_call(functools.partial(factor_kernel, float(total)), grid=(rows...]
  transfers between devices with their start and end apart: 2 -> 0, of which waited for: 1 -> 0; matrix products, arithmetic and copies ran while one was open for 0% -> 0% of each run, Pallas kernels for 0% -> 0%
where the time goes in v2:
time: 132 us; the launch traced here: 131 us
  Pallas kernels  126 us (95%)
  local copies, waits for them, and re-layouts  3.17 us (2%)
  other arithmetic  2.04 us (2%)
    pallas_call x1, Pallas kernels, apply_and_blocks(): pl.pallas_call(apply_kernel, grid=(rows // chunk,), in_specs=[pl.BlockSpe...  49.7 us
    pallas_call x2, Pallas kernels, reduce_tiles(): pl.pallas_call(functools.partial(reduce_kernel, n_grp, n_row), in_specs=[...  35.4 us
    pallas_call x1, Pallas kernels, factor_and_columns(): pl.pallas_call(functools.partial(factor_kernel, float(total)), grid=(rows...  17.8 us
    pallas_call x1, Pallas kernels, exchange(): pl.pallas_call(functools.partial(exchange_kernel, n_grp), in_specs=[pl.Bl...  10.6 us
    pallas_call x1, Pallas kernels, gram_sums(): pl.pallas_call(gram_kernel, grid=(rows // chunk,), in_specs=[pl.BlockSpec...  7.45 us
    pallas_call x1, Pallas kernels, halo(): pl.pallas_call(functools.partial(halo_kernel, n_row, count), in_specs=[vm...  4.7 us

profile of v2, /device:TPU:0, one launch (start us, length us, event | category | flops | bytes accessed | tf_op | source)
XLA Modules:
  0.0 131.5 jit_solution(2199427175642917777)
XLA Ops:
  0.6 0.7 add_bitcast_fusion
  1.3 0.7 copy.12.visc_ref
  2.0 0.0 copy-start.1
  2.0 1.0 copy-done.1
  3.0 10.6 %exchange.1.arrived_ref = f32[16,8192]{1,0:T(8,128)S(1)} custom-call(f32[4,4,8192]{2,1,0:T(4,128)S(1)} %copy-done.1), custom_call_target="tpu_custom_call" | custom-call | tf_op jit(solution)/shard_map/exchange/pallas_call | solution.py:118
  13.7 0.0 copy-start
  13.7 0.8 copy-done
  14.5 7.4 %gram_sums.1 = f32[192,128]{1,0:T(8,128)} custom-call(f32[128,8192]{1,0:T(8,128)} %basis_ref.5, f32[16,8192]{1,0:T(8,128)} %copy-done), custom_call_target="tpu_custom_call" | custom-call | tf_op jit(solution)/shard_map/gram_sums/pallas_call | solution.py:64
  21.9 17.5 %reduce_tiles.2 = f32[8,24,128]{2,1,0:T(8,128)} custom-call(f32[8,24,128]{2,1,0:T(8,128)} %bitcast.16), custom_call_target="tpu_custom_call" | custom-call | tf_op jit(solution)/shard_map/reduce_tiles/pallas_call | solution.py:298
  39.4 17.8 %factor_and_columns.1 = (f32[16,8192]{1,0:T(8,128)}, f32[16,128]{1,0:T(8,128)}, f32[16,16]{1,0:T(8,128)}) custom-call(f32[192,128]{1,0:T(8,128)} %bitcast.15, s32[1,16]{1,0:T(1,128)} %bitcast.19, f32[128,8192]{1,0:T(8,128)} %basis_ref.5, f32[16,8192]{1,0:T(8,128)} %copy-done), custom_call_target="tpu_custom_call" | custom-call | tf_op jit(solution)/shard_map/factor_and_columns/pallas_call | solution.py:382
  57.2 4.7 %halo.1 = (f32[16,2048]{1,0:T(8,128)}, f32[16,2048]{1,0:T(8,128)}) custom-call(f32[16,8192]{1,0:T(8,128)} %get-tuple-element.7.new_ref.mid_ref), custom_call_target="tpu_custom_call" | custom-call | tf_op jit(solution)/shard_map/halo/pallas_call | solution.py:206
  61.9 49.7 %apply_and_blocks.1 = (f32[2,16,8192]{2,1,0:T(8,128)}, f32[64,128]{1,0:T(8,128)}) custom-call(f32[16,2048]{1,0:T(8,128)} %get-tuple-element.14.low_ref, f32[16,8192]{1,0:T(8,128)} %get-tuple-element.7.new_ref.mid_ref, f32[16,2048]{1,0:T(8,128)} %get-tuple-element.15.high_ref, f32[16,1]{1,0:T(8,128)} %copy.12.visc_ref, s32[8,8192]{1,0:T(8,128)} %off_ref.1, ...), custom_call_target="tpu_custom_call" | custom-call | tf_op jit(solution)/shard_map/apply_and_blocks/pallas_call | solution.py:494
  111.6 17.8 %reduce_tiles.3 = f32[8,8,128]{2,1,0:T(8,128)} custom-call(f32[8,8,128]{2,1,0:T(8,128)} %bitcast.18), custom_call_target="tpu_custom_call" | custom-call | tf_op jit(solution)/shard_map/reduce_tiles/pallas_call | solution.py:298
  129.4 0.8 broadcast_multiply_fusion
  130.2 0.1 slice.18
  130.3 0.6 copy.14
  130.9 0.6 pad_maximum_fusion
  (2 shorter events, 0.0 us)
Async XLA Ops:
  2.0 1.0 copy-start.1
  13.7 0.8 copy-start

commit v3 on v2

--- a/solution.py
+++ b/solution.py
@@ -9,6 +9,7 @@
 
 NPARAM = 64
 HALO_BLOCKS = 16
+LANE_SLOTS = 3
 F32 = jnp.float32
 BF16 = jnp.bfloat16
 MESH = pl.DeviceIdType.MESH
@@ -408,14 +409,15 @@
     )(sums, assignment.reshape(1, ns), basis, arrived)
 
 
-def apply_kernel(low_ref, mid_ref, high_ref, visc_ref, off_ref, coef_ref, basis_ref, applied_ref, out_ref, ext, bx, nx, sq):
+def apply_kernel(low_ref, mid_ref, high_ref, visc_ref, off_ref, coef_ref, basis_ref, applied_ref, out_ref, ext, wide, bx, nx, sq):
     step = pl.program_id(0)
     ns, chunk = 16, basis_ref.shape[1]
     nb = basis_ref.shape[0]
     terms, slots = coef_ref.shape[0], coef_ref.shape[1]
     width = low_ref.shape[1] // 128
     count = mid_ref.shape[1] // 128
-    per_step = chunk // 128
+    per_step = chunk // 256
+    halves = ns // 8
 
     @pl.when(step == 0)
     def _():
@@ -424,35 +426,65 @@
             ext[width + count + b] = high_ref[:, b * 128 : (b + 1) * 128]
         for b in range(count):
             ext[width + b] = mid_ref[:, b * 128 : (b + 1) * 128]
+        for ref, start in ((low_ref, 0), (mid_ref, width // 2), (high_ref, (width + count) // 2)):
+            for b in range(ref.shape[1] // 256):
+                wide[start + b] = jnp.concatenate(split(ref[:, b * 256 : (b + 1) * 256]), axis=0)
         bx[...] = jnp.zeros_like(bx)
         nx[...] = jnp.zeros_like(nx)
         sq[...] = jnp.zeros_like(sq)
 
-    lanes = lax.broadcasted_iota(jnp.int32, (slots, 128), 1)
+    lanes = lax.broadcasted_iota(jnp.int32, (slots, 256), 1)
+    depth = lax.broadcasted_iota(jnp.int32, (256, 256), 0)
+
+    def by_lanes(spot, t, first):
+        low_index = lax.bitwise_and(spot, 127)
+        block_index = lax.shift_right_logical(spot, 7)
+        sides = [[] for h in range(halves)]
+        for u in range(2):
+            part = slice(u * 128, (u + 1) * 128)
+            lane = jnp.broadcast_to(low_index[t : t + 1, part], (8, 128))
+            block = jnp.broadcast_to(block_index[t : t + 1, part] - u, (8, 128))
+            picked = [jnp.zeros((8, 128), F32) for h in range(halves)]
+            for b in range(2 * width + 1):
+                same = block == b
+                for h in range(halves):
+                    source = ext[2 * first + u + b, h * 8 : (h + 1) * 8, :]
+                    got = jnp.take_along_axis(source, lane, axis=1, mode="promise_in_bounds")
+                    picked[h] = jnp.where(same, got, picked[h])
+            for h in range(halves):
+                sides[h].append(picked[h])
+        return [jnp.concatenate(side, axis=1) for side in sides]
+
+    def by_product(spot, t, window):
+        low_index = lax.bitwise_and(spot, 255)
+        block = jnp.broadcast_to(lax.shift_right_logical(spot, 8)[t : t + 1, :], (8, 256))
+        chosen = (depth == low_index[t : t + 1, :]).astype(F32).astype(BF16)
+        found = jnp.dot(window, chosen, preferred_element_type=F32)
+        picked = [found[g * 8 : (g + 1) * 8, :] for g in range(2 * halves)]
+        for b in range(1, width + 1):
+            same = block == b
+            for g in range(2 * halves):
+                at = b * 2 * ns + g * 8
+                picked[g] = jnp.where(same, found[at : at + 8, :], picked[g])
+        return [picked[h] + picked[halves + h] for h in range(halves)]
 
     def one(c, carry):
         first = step * per_step + c
-        at = pl.ds(pl.multiple_of(c * 128, 128), 128)
+        at = pl.ds(pl.multiple_of(c * 256, 256), 256)
         spot = off_ref[:, at] + (lanes + width * 128)
-        low_index = lax.bitwise_and(spot, 127)
-        block_index = lax.shift_right_logical(spot, 7)
-        totals = [[jnp.zeros((8, 128), F32) for h in range(ns // 8)] for k in range(terms)]
+        window = wide[pl.ds(first, width + 1)].reshape((width + 1) * 2 * ns, 256)
+        totals = [[jnp.zeros((8, 256), F32) for h in range(halves)] for k in range(terms)]
         for t in range(slots):
-            lane = jnp.broadcast_to(low_index[t : t + 1, :], (8, 128))
-            block = jnp.broadcast_to(block_index[t : t + 1, :], (8, 128))
-            picked = [jnp.zeros((8, 128), F32) for h in range(ns // 8)]
-            for b in range(2 * width + 1):
-                same = block == b
-                for h in range(ns // 8):
-                    source = ext[first + b, h * 8 : (h + 1) * 8, :]
-                    got = jnp.take_along_axis(source, lane, axis=1, mode="promise_in_bounds")
-                    picked[h] = jnp.where(same, got, picked[h])
+            if t < LANE_SLOTS:
+                picked = by_lanes(spot, t, first)
+            else:
+                picked = by_product(spot, t, window)
             for k in range(terms):
                 weight = coef_ref[k, t : t + 1, at]
-                for h in range(ns // 8):
+                for h in range(halves):
                     totals[k][h] = totals[k][h] + weight * picked[h]
         for k in range(terms):
-            for h in range(ns // 8):
+            for h in range(halves):
                 applied_ref[k, h * 8 : (h + 1) * 8, at] = totals[k][h]
         return carry
 
@@ -513,6 +545,7 @@
         ],
         scratch_shapes=[
             pltpu.VMEM((blocks, ns, 128), F32),
+            pltpu.VMEM((blocks // 2, 2 * ns, 256), BF16),
             pltpu.VMEM((2 * terms * ns, 2 * nb), F32),
             pltpu.VMEM((2 * terms * ns, 2 * ns), F32),
             pltpu.VMEM((ns, 1), F32),

time: 132 us -> 106 us (0.80)
  Pallas kernels: 126 us -> 99.5 us
    pallas_call x1, Pallas kernels: 49.7 us -> 23.6 us  [apply_and_blocks(): pl.pallas_call(apply_kernel, grid=(rows // chunk,), in_specs=[pl.BlockSpe...]
where the time goes in v3:
time: 106 us; the launch traced here: 105 us
  Pallas kernels  99.5 us (94%)
  local copies, waits for them, and re-layouts  3.17 us (3%)
  other arithmetic  2.04 us (2%)
    pallas_call x2, Pallas kernels, reduce_tiles(): pl.pallas_call(functools.partial(reduce_kernel, n_grp, n_row), in_specs=[...  35.3 us
    pallas_call x1, Pallas kernels, apply_and_blocks(): pl.pallas_call(apply_kernel, grid=(rows // chunk,), in_specs=[pl.BlockSpe...  23.6 us
    pallas_call x1, Pallas kernels, factor_and_columns(): pl.pallas_call(functools.partial(factor_kernel, float(total)), grid=(rows...  17.8 us
    pallas_call x1, Pallas kernels, exchange(): pl.pallas_call(functools.partial(exchange_kernel, n_grp), in_specs=[pl.Bl...  10.6 us
    pallas_call x1, Pallas kernels, gram_sums(): pl.pallas_call(gram_kernel, grid=(rows // chunk,), in_specs=[pl.BlockSpec...  7.45 us
    pallas_call x1, Pallas kernels, halo(): pl.pallas_call(functools.partial(halo_kernel, n_row, count), in_specs=[vm...  4.7 us
    unnamed x5, local copies, waits for them, and re-layouts  2.41 us

profile of v3, /device:TPU:0, one launch (start us, length us, event | category | flops | bytes accessed | tf_op | source)
XLA Modules:
  0.0 105.4 jit_solution(12299451063700185603)
XLA Ops:
  0.6 0.7 add_bitcast_fusion
  1.3 0.7 copy.12.visc_ref
  2.0 0.0 copy-start.1
  2.0 1.0 copy-done.1
  3.0 10.6 %exchange.1.arrived_ref = f32[16,8192]{1,0:T(8,128)S(1)} custom-call(f32[4,4,8192]{2,1,0:T(4,128)S(1)} %copy-done.1), custom_call_target="tpu_custom_call" | custom-call | tf_op jit(solution)/shard_map/exchange/pallas_call | solution.py:119
  13.7 0.0 copy-start
  13.7 0.8 copy-done
  14.5 7.4 %gram_sums.1 = f32[192,128]{1,0:T(8,128)} custom-call(f32[128,8192]{1,0:T(8,128)} %basis_ref.5, f32[16,8192]{1,0:T(8,128)} %copy-done), custom_call_target="tpu_custom_call" | custom-call | tf_op jit(solution)/shard_map/gram_sums/pallas_call | solution.py:65
  21.9 17.5 %reduce_tiles.2 = f32[8,24,128]{2,1,0:T(8,128)} custom-call(f32[8,24,128]{2,1,0:T(8,128)} %bitcast.16), custom_call_target="tpu_custom_call" | custom-call | tf_op jit(solution)/shard_map/reduce_tiles/pallas_call | solution.py:299
  39.4 17.8 %factor_and_columns.1 = (f32[16,8192]{1,0:T(8,128)}, f32[16,128]{1,0:T(8,128)}, f32[16,16]{1,0:T(8,128)}) custom-call(f32[192,128]{1,0:T(8,128)} %bitcast.15, s32[1,16]{1,0:T(1,128)} %bitcast.19, f32[128,8192]{1,0:T(8,128)} %basis_ref.5, f32[16,8192]{1,0:T(8,128)} %copy-done), custom_call_target="tpu_custom_call" | custom-call | tf_op jit(solution)/shard_map/factor_and_columns/pallas_call | solution.py:383
  57.2 4.7 %halo.1 = (f32[16,2048]{1,0:T(8,128)}, f32[16,2048]{1,0:T(8,128)}) custom-call(f32[16,8192]{1,0:T(8,128)} %get-tuple-element.7.new_ref.mid_ref), custom_call_target="tpu_custom_call" | custom-call | tf_op jit(solution)/shard_map/halo/pallas_call | solution.py:207
  61.9 23.6 %apply_and_blocks.1 = (f32[2,16,8192]{2,1,0:T(8,128)}, f32[64,128]{1,0:T(8,128)}) custom-call(f32[16,2048]{1,0:T(8,128)} %get-tuple-element.14.low_ref, f32[16,8192]{1,0:T(8,128)} %get-tuple-element.7.new_ref.mid_ref, f32[16,2048]{1,0:T(8,128)} %get-tuple-element.15.high_ref, f32[16,1]{1,0:T(8,128)} %copy.12.visc_ref, s32[8,8192]{1,0:T(8,128)} %off_ref.1, ...), custom_call_target="tpu_custom_call" | custom-call | tf_op jit(solution)/shard_map/apply_and_blocks/pallas_call | solution.py:526
  85.5 17.8 %reduce_tiles.3 = f32[8,8,128]{2,1,0:T(8,128)} custom-call(f32[8,8,128]{2,1,0:T(8,128)} %bitcast.18), custom_call_target="tpu_custom_call" | custom-call | tf_op jit(solution)/shard_map/reduce_tiles/pallas_call | solution.py:299
  103.4 0.8 broadcast_multiply_fusion
  104.1 0.1 slice.18
  104.2 0.6 copy.14
  104.8 0.6 pad_maximum_fusion
  (2 shorter events, 0.0 us)
Async XLA Ops:
  2.0 1.0 copy-start.1
  13.7 0.8 copy-start

commit v4 on v3

--- a/solution.py
+++ b/solution.py
@@ -492,10 +492,13 @@
 
     flat = jnp.concatenate([applied_ref[k] for k in range(terms)], axis=0)
     combined = applied_ref[0]
-    power = visc_ref[...]
+    across = 0.5 + visc_ref[...].astype(F32) / NPARAM
+    same = lax.broadcasted_iota(jnp.int32, (ns, ns), 0) == lax.broadcasted_iota(jnp.int32, (ns, ns), 1)
+    viscosity = jnp.sum(jnp.where(same, across, 0.0), axis=1, keepdims=True)
+    power = viscosity
     for k in range(1, terms):
         combined = combined + power * applied_ref[k]
-        power = power * visc_ref[...]
+        power = power * viscosity
     sq[...] += jnp.sum(combined * combined, axis=1, keepdims=True)
     y = jnp.concatenate(split(flat), axis=0)
     x = jnp.concatenate(split(basis_ref[...]), axis=0)
@@ -530,7 +533,7 @@
             pl.BlockSpec((ns, width), whole),
             pl.BlockSpec((ns, rows), whole),
             pl.BlockSpec((ns, width), whole),
-            pl.BlockSpec((ns, 1), whole),
+            pl.BlockSpec((1, ns), whole),
             pl.BlockSpec((slots, chunk), lambda i: (0, i)),
             pl.BlockSpec((terms, slots, chunk), lambda i: (0, 0, i)),
             pl.BlockSpec((nb, chunk), lambda i: (0, i)),
@@ -563,10 +566,10 @@
     total = local * devices
     width = HALO_BLOCKS * 128
     arrived = exchange(snapshots)
-    sums = reduce_tiles(gram_sums(basis, arrived, 1024), 1)
+    sums = reduce_tiles(gram_sums(basis, arrived, 2048), 1)
     new, coords_t, r_factor = factor_and_columns(sums, assignment, basis, arrived, total, 2048)
     low, high = halo(new, width)
-    viscosity = (0.5 + param_index.astype(F32) / NPARAM).reshape(ns, 1)
+    viscosity = param_index.reshape(1, ns)
     applied, parts = apply_and_blocks(low, new, high, viscosity, offsets, coefs, basis, 1024)
     parts = reduce_tiles(parts, 2) / total
     f = terms * ns

time: 106 us -> 103 us (0.972)
  Pallas kernels: 99.5 us -> 97.7 us
    pallas_call x1, Pallas kernels: 7.45 us -> 5.59 us  [gram_sums(): pl.pallas_call(gram_kernel, grid=(rows // chunk,), in_specs=[pl.BlockSpec...]
where the time goes in v4:
time: 103 us; the launch traced here: 102 us
  Pallas kernels  97.7 us (95%)
  local copies, waits for them, and re-layouts  2.49 us (2%)
  other arithmetic  1.38 us (1%)
    pallas_call x2, Pallas kernels, reduce_tiles(): pl.pallas_call(functools.partial(reduce_kernel, n_grp, n_row), in_specs=[...  35.3 us
    pallas_call x1, Pallas kernels, apply_and_blocks(): pl.pallas_call(apply_kernel, grid=(rows // chunk,), in_specs=[pl.BlockSpe...  23.6 us
    pallas_call x1, Pallas kernels, factor_and_columns(): pl.pallas_call(functools.partial(factor_kernel, float(total)), grid=(rows...  17.8 us
    pallas_call x1, Pallas kernels, exchange(): pl.pallas_call(functools.partial(exchange_kernel, n_grp), in_specs=[pl.Bl...  10.6 us
    pallas_call x1, Pallas kernels, gram_sums(): pl.pallas_call(gram_kernel, grid=(rows // chunk,), in_specs=[pl.BlockSpec...  5.59 us
    pallas_call x1, Pallas kernels, halo(): pl.pallas_call(functools.partial(halo_kernel, n_row, count), in_specs=[vm...  4.7 us
    unnamed x5, local copies, waits for them, and re-layouts  2.41 us

profile of v4, /device:TPU:0, one launch (start us, length us, event | category | flops | bytes accessed | tf_op | source)
XLA Modules:
  0.0 102.2 jit_solution(15517479031844347913)
XLA Ops:
  0.6 0.0 copy-start.1
  0.6 1.0 %copy-done.1 = f32[4,4,8192]{2,1,0:T(4,128)S(1)} copy-done((f32[4,4,8192]{2,1,0:T(4,128)S(1)}, f32[4,4,8192]{2,1,0:T(4,128)}, u32[]{:S(2)}) %copy-start.1) | copy-done | bytes 524312
  1.7 10.6 %exchange.1.arrived_ref = f32[16,8192]{1,0:T(8,128)S(1)} custom-call(f32[4,4,8192]{2,1,0:T(4,128)S(1)} %copy-done.1), custom_call_target="tpu_custom_call" | custom-call | tf_op jit(solution)/shard_map/exchange/pallas_call | solution.py:119
  12.3 0.0 copy-start
  12.3 0.8 copy-done
  13.1 5.6 %gram_sums.1 = f32[192,128]{1,0:T(8,128)} custom-call(f32[128,8192]{1,0:T(8,128)} %basis_ref.5, f32[16,8192]{1,0:T(8,128)} %copy-done), custom_call_target="tpu_custom_call" | custom-call | tf_op jit(solution)/shard_map/gram_sums/pallas_call | solution.py:65
  18.7 17.5 %reduce_tiles.2 = f32[8,24,128]{2,1,0:T(8,128)} custom-call(f32[8,24,128]{2,1,0:T(8,128)} %bitcast.15), custom_call_target="tpu_custom_call" | custom-call | tf_op jit(solution)/shard_map/reduce_tiles/pallas_call | solution.py:299
  36.2 17.8 %factor_and_columns.1 = (f32[16,8192]{1,0:T(8,128)}, f32[16,128]{1,0:T(8,128)}, f32[16,16]{1,0:T(8,128)}) custom-call(f32[192,128]{1,0:T(8,128)} %bitcast.14, s32[1,16]{1,0:T(1,128)} %bitcast.18, f32[128,8192]{1,0:T(8,128)} %basis_ref.5, f32[16,8192]{1,0:T(8,128)} %copy-done), custom_call_target="tpu_custom_call" | custom-call | tf_op jit(solution)/shard_map/factor_and_columns/pallas_call | solution.py:383
  54.0 4.7 %halo.1 = (f32[16,2048]{1,0:T(8,128)}, f32[16,2048]{1,0:T(8,128)}) custom-call(f32[16,8192]{1,0:T(8,128)} %get-tuple-element.7.new_ref.mid_ref), custom_call_target="tpu_custom_call" | custom-call | tf_op jit(solution)/shard_map/halo/pallas_call | solution.py:207
  58.7 23.6 %apply_and_blocks.1 = (f32[2,16,8192]{2,1,0:T(8,128)}, f32[64,128]{1,0:T(8,128)}) custom-call(f32[16,2048]{1,0:T(8,128)} %get-tuple-element.14.low_ref, f32[16,8192]{1,0:T(8,128)} %get-tuple-element.7.new_ref.mid_ref, f32[16,2048]{1,0:T(8,128)} %get-tuple-element.15.high_ref, s32[1,16]{1,0:T(1,128)} %bitcast.19, s32[8,8192]{1,0:T(8,128)} %off_ref.1, ...), custom_call_target="tpu_custom_call" | custom-call | tf_op jit(solution)/shard_map/apply_and_blocks/pallas_call | solution.py:529
  82.4 17.8 %reduce_tiles.3 = f32[8,8,128]{2,1,0:T(8,128)} custom-call(f32[8,8,128]{2,1,0:T(8,128)} %bitcast.17), custom_call_target="tpu_custom_call" | custom-call | tf_op jit(solution)/shard_map/reduce_tiles/pallas_call | solution.py:299
  100.2 0.8 broadcast_multiply_fusion
  101.0 0.1 slice.18
  101.0 0.6 copy.13
  101.6 0.6 pad_maximum_fusion
  (2 shorter events, 0.0 us)
Async XLA Ops:
  0.6 1.0 %copy-start.1 = (f32[4,4,8192]{2,1,0:T(4,128)S(1)}, f32[4,4,8192]{2,1,0:T(4,128)}, u32[]{:S(2)}) copy-start(f32[4,4,8192]{2,1,0:T(4,128)} %snap_ref.1) | copy-start | bytes 1572868
  12.3 0.8 copy-start
